TPU v7x, 256 devices: a whole 4x4x8 slice. The times are simulated.
256 devices in a mesh: section: 8 (over x, y_lo), seq: 32 (over z, y_hi, core).
Axes of the slice: x: 4, y: 4 (y_hi: 2, y_lo: 2; y = y_hi * 2 + y_lo), z: 8, core: 2. Of those that a mesh axis runs over, the one named last changes fastest.
Arguments:
- queries: bfloat16 [8, 4096, 4096], P('section', 'seq'), may hold values from -6 to 6
- key_rows: bfloat16 [8, 4096, 512], P('section', 'seq'), may hold values from -6 to 6
- value_rows: bfloat16 [8, 4096, 512], P('section', 'seq'), may hold values from -6 to 6
- upstream: bfloat16 [8, 4096, 4096], P('section', 'seq'), may hold values from -6 to 6
- norm_gains: float32 [8, 256], P('section'), may hold values from 0.5 to 8, as said below
- segments: int32 [8, 4096], P('section'), may hold values from 0 to 5, never falling along the last dimension, each value on 1 to 1024 neighbouring positions
Outputs:
- attended: bfloat16 [8, 4096, 4096], P('section', 'seq')
- grad_queries: bfloat16 [8, 4096, 4096], P('section', 'seq')
- grad_keys: bfloat16 [8, 4096, 512], P('section', 'seq')
- grad_values: bfloat16 [8, 4096, 512], P('section', 'seq')
- grad_gains: float32 [8, 256], P('section')
Inputs may be any that keep to these rules, and one draw needn't show every extreme that they name: `norm_gains`: row g of the gains equals row 7 - g. `segments`: document numbers never fall along a slab; a document spans at most 1024 tokens of it.
All inputs are finite; a program needn't handle non-finite values.
Results may differ from a plain program's by a relative error of at most 0.033.
The roundings to bfloat16 on the way count: a program that leaves them out, or rounds other values in their place, can miss the bound.
Values may be sent and summed in bfloat16 or wider, within the bound.
A program may use at most 128 MiB of HBM per device.

v0:
```python
import functools
import math

import jax
import jax.numpy as jnp
from jax import lax
from jax.experimental import pallas as pl
from jax.experimental.pallas import tpu as pltpu
from jax.sharding import PartitionSpec as P

MESH = pl.DeviceIdType.MESH
HEAD_DIM = 128
GROUP = 8
ROWS = 128
PAIR = 2 * ROWS
SLOTS = 5
SPAN = SLOTS * PAIR
SEEN = SPAN - ROWS
EPSILON = 1e-06
FACTOR = 1.0 / math.sqrt(HEAD_DIM)
EXP2_FACTOR = FACTOR * math.log2(math.e)
MASKED = -1e30
F32 = jnp.float32
BF16 = jnp.bfloat16


def matmul(left, right, left_dim, right_dim):
    return lax.dot_general(
        left, right, (((left_dim,), (right_dim,)), ((), ())), preferred_element_type=F32
    )


def unit_rows(raw):
    values = raw.astype(F32)
    inverse = lax.rsqrt(jnp.mean(values * values, axis=-1, keepdims=True) + EPSILON)
    return values * inverse, inverse


def at_slot(slot):
    return pl.ds(pl.multiple_of(slot * PAIR, PAIR), PAIR)


def kernel(
    queries, keys, values, upstream, gains, segments,
    attended, grad_q, grad_k, grad_v, grad_gains,
    q_raw, up_raw, kv_raw, q_normed, k_normed, k_unit_t, bias, acc,
    out_stage, kv_stage, sum_out, sum_in, gain_acc, gain_a, gain_b,
    local_sem, core_send, core_recv, gather_send, gather_recv,
    reduce_send, reduce_recv, out_sem, out_send, out_recv,
    kv_sem, kv_send, kv_recv, ga_send, ga_recv, gb_send, gb_recv,
):
    section = lax.axis_index("section")
    place = lax.axis_index("seq")
    core = place % 2
    col = (place // 2) % 2
    z = place // 4
    mirror = section // 4
    z_count = 8
    other = 1 - core
    gain_q = gains[:, :HEAD_DIM]
    gain_k = gains[:, HEAD_DIM:]

    def device(z_at, col_at, core_at, section_at=None):
        return (section if section_at is None else section_at, (z_at * 2 + col_at) * 2 + core_at)

    sibling = device(z, col, 1 - core)
    across = device(z, 1 - col, core)
    up_z = device((z + 1) % z_count, col, core)
    down_z = device((z + z_count - 1) % z_count, col, core)
    slant_up = device((z + col) % z_count, 1 - col, core)
    slant_down = device((z + z_count + col - 1) % z_count, 1 - col, core)
    slant = device((z + z_count + 2 * col - 1) % z_count, 1 - col, core)

    up_cross = device((z + 1) % z_count, col, other)
    down_cross = device((z + z_count - 1) % z_count, col, other)

    def z_peer(step):
        return device((z + step) % z_count, col, core)

    def square_peer(code):
        flip_m, flip_h, flip_c = code // 4, (code // 2) % 2, code % 2
        return device(
            z,
            1 - col if flip_h else col,
            1 - core if flip_c else core,
            7 - section if flip_m else section,
        )

    barrier = pltpu.get_barrier_semaphore()
    for step in range(1, 8):
        pl.semaphore_signal(barrier, inc=1, device_id=square_peer(step), device_id_type=MESH)
    for step in range(1, 8):
        pl.semaphore_signal(barrier, inc=1, device_id=z_peer(step), device_id_type=MESH)
    for peer in (slant, up_cross, down_cross):
        pl.semaphore_signal(barrier, inc=1, device_id=peer, device_id_type=MESH)

    def remote(src, dst, send, recv, target):
        return pltpu.make_async_remote_copy(
            src_ref=src, dst_ref=dst, send_sem=send, recv_sem=recv,
            device_id=target, device_id_type=MESH,
        )

    def q_columns(core_at, j):
        return pl.ds(pl.multiple_of(core_at * 2048 + j * 1024, 1024), 1024)

    def kv_columns(core_at, j):
        return pl.ds(pl.multiple_of(core_at * 256 + j * 128, 128), 128)

    def token_rows(core_at):
        return pl.ds(pl.multiple_of((SLOTS - 1) * PAIR + core_at * ROWS, ROWS), ROWS)

    def landing(kind, j):
        if kind < 2:
            return kv_raw.at[j, kind, token_rows(core), :]
        return (q_raw, up_raw)[kind - 2].at[core, :, pl.ds(j * 1024, 1024)]

    def leaving(kind, j, core_at):
        if kind < 2:
            return (keys, values)[kind].at[0, :, kv_columns(core_at, j)]
        return (queries, upstream)[kind - 2].at[0, :, q_columns(core_at, j)]

    def own_copy(kind, j):
        return pltpu.make_async_copy(
            leaving(kind, j, core), landing(kind, j), local_sem.at[kind, j]
        )

    def core_copy(kind, j):
        return remote(
            leaving(kind, j, other), landing(kind, j),
            core_send.at[kind, j], core_recv.at[kind, j], sibling,
        )

    def gather_copy(j, kind, step):
        if step < 2:
            source, target_slot, target = 4 - 2 * step, 2 - 2 * step, up_z
        elif step == 2:
            source, target_slot, target = 4 - 2 * col, 3, across
        else:
            source, target_slot, target = 2, 1, slant_up
        return remote(
            kv_raw.at[j, kind, at_slot(source), :],
            kv_raw.at[j, kind, at_slot(target_slot), :],
            gather_send.at[j, kind, step],
            gather_recv.at[j, kind, step],
            target,
        )

    def head_columns(j):
        return [
            slice((j * GROUP + head) * HEAD_DIM, (j * GROUP + head + 1) * HEAD_DIM)
            for head in range(GROUP)
        ]

    def stacked(ref, r, j):
        return jnp.concatenate([ref[r, :, at] for at in head_columns(j)], 0)

    def prepare_queries(j, r):
        unit, _ = unit_rows(stacked(q_raw, r, j))
        q_normed[j, r] = (unit * gain_q).astype(BF16)

    def prepare_keys(j, slot):
        rows = slice(slot * PAIR, (slot + 1) * PAIR)
        unit, _ = unit_rows(kv_raw[j, 0, rows, :])
        k_normed[j, rows, :] = (unit * gain_k).astype(BF16)
        k_unit_t[j, :, rows] = unit.T

    for kind in (2, 0, 1, 3):
        for j in range(2):
            own_copy(kind, j).start()

    pair_at = z * 2 + col
    pieces = []
    for piece in range(SPAN // 128):
        at = jnp.maximum(pair_at * 2 - 8 + piece, 0)
        pieces.append(segments[:, pl.ds(pl.multiple_of(at * 128, 128), 128)].astype(F32))
    row_at = lax.broadcasted_iota(jnp.int32, (ROWS, SEEN), 0)
    key_at = lax.broadcasted_iota(jnp.int32, (ROWS, SEEN), 1)
    diagonal = lax.broadcasted_iota(jnp.int32, (ROWS, ROWS), 0) == lax.broadcasted_iota(
        jnp.int32, (ROWS, ROWS), 1
    )
    for r in range(2):
        row_segments = jnp.sum(jnp.where(diagonal, pieces[8 + r], 0.0), axis=1, keepdims=True)
        key_segments = jnp.concatenate(pieces[r : r + 9], axis=1)
        first_key = 1024 - r * ROWS - (pair_at % 8) * PAIR
        allowed = (
            (key_at <= row_at + 1024) & (key_at >= first_key) & (key_segments == row_segments)
        )
        bias[r] = jnp.where(allowed, 0.0, MASKED)
    acc[...] = jnp.zeros_like(acc)
    gain_acc[...] = jnp.zeros_like(gain_acc)
    for j in range(2):
        own_copy(2, j).wait()
        prepare_queries(j, core)

    def first_copy(kind, cross):
        rows = pl.ds(pl.multiple_of(2 * PAIR + core * ROWS, ROWS), ROWS)
        return remote(
            leaving(kind, 0, other if cross else core),
            kv_raw.at[0, kind, rows, :],
            gather_send.at[0, kind, 4 * cross],
            gather_recv.at[0, kind, 4 * cross],
            up_cross if cross else up_z,
        )

    def enter(j, kind):
        own_copy(kind, j).wait()
        core_copy(kind, j).wait_recv()
        if j == 1:
            gather_copy(j, kind, 0).start()

    def pass_on(j, kind):
        if j == 0:
            first_copy(kind, 0).wait_recv()
            first_copy(kind, 1).wait_recv()
        else:
            gather_copy(j, kind, 0).wait_recv()
        gather_copy(j, kind, 1).start()
        gather_copy(j, kind, 3).start()

    pl.semaphore_wait(barrier, 17)
    for kind in range(2):
        for cross in range(2):
            first_copy(kind, cross).start()
    for j in range(2):
        for kind in range(2):
            core_copy(kind, j).start()
    for j in range(2):
        for kind in range(2, 4):
            core_copy(kind, j).start()
    for kind in range(2):
        enter(0, kind)

        @pl.when(col == 0)
        def _():
            gather_copy(0, kind, 2).start()

    prepare_keys(0, 4)
    pass_on(0, 0)

    @pl.when(col == 1)
    def _():
        gather_copy(0, 0, 2).start()

    enter(1, 0)
    pass_on(0, 1)

    @pl.when(col == 1)
    def _():
        gather_copy(0, 1, 2).start()

    enter(1, 1)
    prepare_keys(0, 2)
    prepare_keys(1, 4)
    core_copy(2, 0).wait_recv()
    prepare_queries(0, other)
    core_copy(2, 1).wait_recv()
    prepare_queries(1, other)

    def reduce_copy(j, kind, step):
        target = (down_z, down_z, across, slant_down)[step]
        return remote(
            sum_out.at[j, kind, step],
            sum_in.at[j, kind, step],
            reduce_send.at[j, kind, step],
            reduce_recv.at[j, kind, step],
            target,
        )

    def send_sum(j, kind, step, slot):
        sum_out[j, kind, step] = acc[j, kind, :, at_slot(slot)].astype(BF16)
        reduce_copy(j, kind, step).start()

    def add_sum(j, kind, step, slot):
        reduce_copy(j, kind, step).wait_recv()
        acc[j, kind, :, at_slot(slot)] += sum_in[j, kind, step].astype(F32)

    def reduce_first(j, kind):
        send_sum(j, kind, 3, 1)
        send_sum(j, kind, 0, 0)
        send_sum(j, kind, 2, 3)

    def reduce_second(j, kind):
        add_sum(j, kind, 3, 2)
        add_sum(j, kind, 0, 2)
        add_sum(j, kind, 2, 4 - 2 * col)
        send_sum(j, kind, 1, 2)

    def kv_copy(kind, j, r):
        target = (grad_k, grad_v)[kind].at[0, :, kv_columns(core, j)]
        if r is core:
            return pltpu.make_async_copy(kv_stage.at[j, kind, r], target, kv_sem.at[j, kind])
        return remote(
            kv_stage.at[j, kind, r], target, kv_send.at[j, kind], kv_recv.at[j, kind], sibling
        )

    def reduce_last(j, kind):
        add_sum(j, kind, 1, 4)
        slot = at_slot(SLOTS - 1)
        result = acc[j, kind, :, slot].T
        if kind == 0:
            k_unit, k_inverse = unit_rows(kv_raw[j, 0, slot, :])
            scaled = result * gain_k
            result = (
                scaled - k_unit * jnp.mean(scaled * k_unit, axis=-1, keepdims=True)
            ) * k_inverse
        kv_stage[j, kind] = result.astype(BF16).reshape(2, ROWS, HEAD_DIM)
        kv_copy(kind, j, other).start()
        kv_copy(kind, j, core).start()

    def out_copy(kind, j, r):
        target = (attended, grad_q)[kind].at[0, :, q_columns(core, j)]
        source = out_stage.at[kind, r, :, pl.ds(j * 1024, 1024)]
        if r is core:
            return pltpu.make_async_copy(source, target, out_sem.at[kind, j])
        return remote(source, target, out_send.at[kind, j], out_recv.at[kind, j], sibling)

    def attend(j, before_values, after_values, after_keys, after_gains):
        both = range(2)
        seen = [slice(r * ROWS, r * ROWS + SEEN) for r in both]
        q = [q_normed[j, r] for r in both]
        k = [k_normed[j, seen[r], :] for r in both]
        scores, d_probs, probs, probs_b, delta, d_scores = ([None, None] for _ in range(6))

        up = v = None

        def softmax(r):
            masked = scores[r].reshape(GROUP, ROWS, SEEN) + bias[r][None]
            masked = masked.reshape(GROUP * ROWS, SEEN)
            top = jnp.max(masked, axis=1, keepdims=True)
            weights = jnp.exp2((masked - top) * EXP2_FACTOR)
            probs[r] = weights * (1.0 / jnp.sum(weights, axis=1, keepdims=True))
            probs_b[r] = probs[r].astype(BF16)

        def output(r):
            out = matmul(probs_b[r], v[r], 1, 0).astype(BF16)
            delta[r] = jnp.sum(up[r].astype(F32) * out.astype(F32), axis=1, keepdims=True)
            for head, at in enumerate(head_columns(j)):
                out_stage[0, r, :, at] = out[head * ROWS : (head + 1) * ROWS]

        def score_gradient(r):
            d_scores[r] = (probs[r] * (d_probs[r] - delta[r]) * FACTOR).astype(BF16)

        def query_gradient(r):
            d_qn = matmul(d_scores[r], k[r], 1, 0).astype(BF16).astype(F32)
            q_unit, q_inverse = unit_rows(stacked(q_raw, r, j))
            gain_acc[0] += jnp.sum((d_qn * q_unit).reshape(ROWS, GROUP, HEAD_DIM), axis=0)
            scaled = d_qn * gain_q
            d_query = (
                (scaled - q_unit * jnp.mean(scaled * q_unit, axis=-1, keepdims=True)) * q_inverse
            ).astype(BF16)
            for head, at in enumerate(head_columns(j)):
                out_stage[1, r, :, at] = d_query[head * ROWS : (head + 1) * ROWS]

        for r in both:
            scores[r] = matmul(q[r], k[r], 1, 1)
        softmax(0)
        before_values()
        up = [stacked(up_raw, r, j) for r in both]
        v = [kv_raw[j, 1, seen[r], :] for r in both]
        d_probs[0] = matmul(up[0], v[0], 1, 1)
        softmax(1)
        output(0)
        score_gradient(0)
        acc[j, 1, :, seen[0]] += matmul(up[0], probs_b[0], 0, 0)
        d_probs[1] = matmul(up[1], v[1], 1, 1)
        output(1)
        acc[j, 1, :, seen[1]] += matmul(up[1], probs_b[1], 0, 0)
        after_values()
        score_gradient(1)
        acc[j, 0, :, seen[0]] += matmul(q[0], d_scores[0], 0, 0)
        acc[j, 0, :, seen[1]] += matmul(q[1], d_scores[1], 0, 0)
        after_keys()
        query_gradient(0)
        query_gradient(1)
        product = acc[j, 0] * k_unit_t[j]
        total = product[:, :128]
        for piece in range(1, SPAN // 128):
            total = total + product[:, piece * 128 : (piece + 1) * 128]
        gain_acc[1] += jnp.sum(total.T.reshape(16, 8, HEAD_DIM), axis=0)
        after_gains()
        for kind in (1, 0):
            out_copy(kind, j, other).start()
            out_copy(kind, j, core).start()

    def arrive(j, kind, slots=()):
        for step in range(1, 4):
            gather_copy(j, kind, step).wait_recv()
        for slot in slots:
            prepare_keys(j, slot)

    def pass_across(kind):
        pass_on(1, kind)
        gather_copy(1, kind, 2).start()

    def first_values():
        own_copy(3, 0).wait()
        core_copy(3, 0).wait_recv()
        pass_across(0)
        arrive(0, 1)

    def second_values():
        own_copy(3, 1).wait()
        core_copy(3, 1).wait_recv()
        arrive(1, 1)

    def gain_a_copy(step):
        return remote(
            gain_a.at[0], gain_a.at[step], ga_send.at[step], ga_recv.at[step], z_peer(step)
        )

    def gain_b_copy(code):
        return remote(
            gain_b.at[0], gain_b.at[code], gb_send.at[code], gb_recv.at[code], square_peer(code)
        )

    def send_gains():
        gain_a[0, 0:1] = jnp.sum(gain_acc[0], axis=0, keepdims=True)
        gain_a[0, 1:2] = jnp.sum(gain_acc[1], axis=0, keepdims=True)
        gain_a[0, 2:8] = jnp.zeros((6, HEAD_DIM), F32)
        for at in range(1, 8):
            gain_a_copy(at).start()

    def nothing():
        pass

    def first_sums():
        reduce_first(0, 1)
        reduce_first(0, 0)

    def value_sums():
        reduce_second(0, 1)
        reduce_first(1, 1)

    def key_sums():
        reduce_first(1, 0)
        reduce_second(0, 0)

    arrive(0, 0, (0, 1, 3))
    attend(0, first_values, lambda: pass_across(1), first_sums, nothing)
    arrive(1, 0, (0, 1, 2, 3))
    attend(1, second_values, value_sums, key_sums, send_gains)
    reduce_last(0, 1)
    reduce_second(1, 1)
    reduce_last(0, 0)
    reduce_second(1, 0)
    for at in range(1, 8):
        gain_a_copy(at).wait_recv()
    terms = gain_a[z % 8]
    for at in range(1, 8):
        terms = terms + gain_a[(z + 8 - at) % 8]
    gain_b[0] = terms
    for at in range(1, 8):
        gain_b_copy(at).start()
    reduce_last(1, 1)
    reduce_last(1, 0)
    for at in range(1, 8):
        gain_b_copy(at).wait_recv()
    sums = []
    for m in range(2):
        total = None
        for h in range(2):
            for c in range(2):
                term = gain_b[((mirror + m) % 2) * 4 + ((col + h) % 2) * 2 + (core + c) % 2]
                total = term if total is None else total + term
        sums.append(total)
    result = sums[0] + sums[1]
    grad_gains[:, :HEAD_DIM] = result[0:1]
    grad_gains[:, HEAD_DIM:] = result[1:2]

    for j in range(2):
        for kind in range(4):
            core_copy(kind, j).wait_send()
        for kind in range(2):
            for at in range(4):
                if j == 0 and at == 0:
                    first_copy(kind, 0).wait_send()
                    first_copy(kind, 1).wait_send()
                else:
                    gather_copy(j, kind, at).wait_send()
                reduce_copy(j, kind, at).wait_send()
            out_copy(kind, j, core).wait()
            out_copy(kind, j, other).wait()
            kv_copy(kind, j, core).wait()
            kv_copy(kind, j, other).wait()
    for at in range(1, 8):
        gain_a_copy(at).wait_send()
        gain_b_copy(at).wait_send()


def hand_over(*refs):
    sources, targets, buffers, (in_sem, out_sem) = refs[:5], refs[5:10], refs[10:15], refs[15:]
    ways = []
    for at, (source, target, buffer) in enumerate(zip(sources, targets, buffers)):
        pieces = 4 if at < 2 else 1
        for piece in range(pieces):
            if len(source.shape) == 3:
                count = source.shape[1] // pieces
                view = (0, pl.ds(piece * count, count))
            else:
                view = (pl.ds(0, 1),)
            ways.append(
                (
                    pltpu.make_async_copy(
                        source.at[view], buffer.at[view], in_sem.at[at * 4 + piece]
                    ),
                    pltpu.make_async_copy(
                        buffer.at[view], target.at[view], out_sem.at[at * 4 + piece]
                    ),
                )
            )
    for inward, _ in ways:
        inward.start()
    for inward, outward in ways:
        inward.wait()
        outward.start()
    for _, outward in ways:
        outward.wait()


def on_device(queries, key_rows, value_rows, upstream, norm_gains, segments):
    any_space = pl.BlockSpec(memory_space=pl.ANY)
    vmem = pl.BlockSpec(memory_space=pltpu.VMEM)
    dma = pltpu.SemaphoreType.DMA
    shapes = [
        jax.ShapeDtypeStruct(queries.shape, BF16),
        jax.ShapeDtypeStruct(queries.shape, BF16),
        jax.ShapeDtypeStruct(key_rows.shape, BF16),
        jax.ShapeDtypeStruct(key_rows.shape, BF16),
        jax.ShapeDtypeStruct(norm_gains.shape, F32),
    ]
    results = pl.pallas_call(
        kernel,
        out_shape=shapes,
        in_specs=[any_space] * 4 + [vmem] * 2,
        out_specs=[any_space] * 4 + [vmem],
        scratch_shapes=[
            pltpu.VMEM((2, ROWS, 2048), BF16),
            pltpu.VMEM((2, ROWS, 2048), BF16),
            pltpu.VMEM((2, 2, SPAN, HEAD_DIM), BF16),
            pltpu.VMEM((2, 2, GROUP * ROWS, HEAD_DIM), BF16),
            pltpu.VMEM((2, SPAN, HEAD_DIM), BF16),
            pltpu.VMEM((2, HEAD_DIM, SPAN), F32),
            pltpu.VMEM((2, ROWS, SEEN), F32),
            pltpu.VMEM((2, 2, HEAD_DIM, SPAN), F32),
            pltpu.VMEM((2, 2, ROWS, 2048), BF16),
            pltpu.VMEM((2, 2, 2, ROWS, HEAD_DIM), BF16),
            pltpu.VMEM((2, 2, 4, HEAD_DIM, PAIR), BF16),
            pltpu.VMEM((2, 2, 4, HEAD_DIM, PAIR), BF16),
            pltpu.VMEM((2, 8, HEAD_DIM), F32),
            pltpu.VMEM((8, 8, HEAD_DIM), F32),
            pltpu.VMEM((8, 8, HEAD_DIM), F32),
            dma((4, 2)),
            dma((4, 2)),
            dma((4, 2)),
            dma((2, 2, 5)),
            dma((2, 2, 5)),
            dma((2, 2, 4)),
            dma((2, 2, 4)),
            dma((2, 2)),
            dma((2, 2)),
            dma((2, 2)),
            dma((2, 2)),
            dma((2, 2)),
            dma((2, 2)),
            dma((8,)),
            dma((8,)),
            dma((8,)),
            dma((8,)),
        ],
        compiler_params=pltpu.CompilerParams(
            collective_id=0, has_side_effects=True, vmem_limit_bytes=60 * 2**20
        ),
        cost_estimate=pl.CostEstimate(
            flops=6 * 10**9, bytes_accessed=5 * 10**6, transcendentals=5 * 10**6
        ),
    )(queries, key_rows, value_rows, upstream, norm_gains, segments)
    return tuple(
        pl.pallas_call(
            hand_over,
            out_shape=shapes,
            in_specs=[any_space] * 5,
            out_specs=[any_space] * 5,
            scratch_shapes=[pltpu.VMEM(one.shape, one.dtype) for one in shapes]
            + [dma((20,)), dma((20,))],
        )(*results)
    )


def solution(mesh):
    rows = P("section", "seq", None)
    whole = P("section", None)
    return jax.shard_map(
        on_device,
        mesh=mesh,
        in_specs=(rows, rows, rows, rows, whole, whole),
        out_specs=(rows, rows, rows, rows, whole),
        check_vma=False,
    )
```

profile of v0, /device:TPU:1, one launch (start us, length us, event | category | flops | bytes accessed | tf_op | source)
XLA Modules:
  0.0 62.1 jit_solution(10068184217484379883)
XLA Ops:
  0.6 58.6 %shard_map.101 = (bf16[1,128,4096]{2,1,0:T(8,128)(2,1)}, bf16[1,128,4096]{2,1,0:T(8,128)(2,1)}, bf16[1,128,512]{2,1,0:T(8,128)(2,1)}, bf16[1,128,512]{2,1,0:T(8,128)(2,1)}, f32[1,256]{1,0:T(1,128)}) custom-call(bf16[1,128,4096]{2,1,0:T(8,128)(2,1)} %queries.1, bf16[1,128,512]{2,1,0:T(8,128)(2,1)} %keys.1, bf16[1,128,512]{2,1,0:T(8,128)(2,1)} %values.1, ...), custom_call_target="tpu_custom_call" | custom-call | flops 6000000000 | bytes 5000000 | tf_op jit(solution)/shard_map/pallas_call | solution.py:531
  59.2 2.7 %shard_map.102 = (bf16[1,128,4096]{2,1,0:T(8,128)(2,1)}, bf16[1,128,4096]{2,1,0:T(8,128)(2,1)}, bf16[1,128,512]{2,1,0:T(8,128)(2,1)}, bf16[1,128,512]{2,1,0:T(8,128)(2,1)}, f32[1,256]{1,0:T(1,128)}) custom-call(bf16[1,128,4096]{2,1,0:T(8,128)(2,1)} %get-tuple-element.10.refs_0_, bf16[1,128,4096]{2,1,0:T(8,128)(2,1)} %get-tuple-element.11.refs_1_, ...), custom_call_target="tpu_custom_call" | custom-call | tf_op jit(solution)/shard_map/pallas_call | solution.py:578
where the time goes:
time: 62.2 us; the launch traced here: 62.1 us
  Pallas kernels  61.3 us (99%)
  between operations  0.8 us (1%)
    pallas_call x1, Pallas kernels, on_device(): pl.pallas_call(kernel, out_shape=shapes, in_specs=[any_space] * 4 + [vmem...  58.6 us
    pallas_call x1, Pallas kernels, on_device(): pl.pallas_call(hand_over, out_shape=shapes, in_specs=[any_space] * 5, out...  2.69 us

commit v1 on v0

--- a/solution.py
+++ b/solution.py
@@ -487,36 +487,6 @@
         gain_b_copy(at).wait_send()
 
 
-def hand_over(*refs):
-    sources, targets, buffers, (in_sem, out_sem) = refs[:5], refs[5:10], refs[10:15], refs[15:]
-    ways = []
-    for at, (source, target, buffer) in enumerate(zip(sources, targets, buffers)):
-        pieces = 4 if at < 2 else 1
-        for piece in range(pieces):
-            if len(source.shape) == 3:
-                count = source.shape[1] // pieces
-                view = (0, pl.ds(piece * count, count))
-            else:
-                view = (pl.ds(0, 1),)
-            ways.append(
-                (
-                    pltpu.make_async_copy(
-                        source.at[view], buffer.at[view], in_sem.at[at * 4 + piece]
-                    ),
-                    pltpu.make_async_copy(
-                        buffer.at[view], target.at[view], out_sem.at[at * 4 + piece]
-                    ),
-                )
-            )
-    for inward, _ in ways:
-        inward.start()
-    for inward, outward in ways:
-        inward.wait()
-        outward.start()
-    for _, outward in ways:
-        outward.wait()
-
-
 def on_device(queries, key_rows, value_rows, upstream, norm_gains, segments):
     any_space = pl.BlockSpec(memory_space=pl.ANY)
     vmem = pl.BlockSpec(memory_space=pltpu.VMEM)
@@ -530,9 +500,9 @@
     ]
     results = pl.pallas_call(
         kernel,
-        out_shape=shapes,
+        out_shape=[pltpu.VMEM(one.shape, one.dtype) for one in shapes],
         in_specs=[any_space] * 4 + [vmem] * 2,
-        out_specs=[any_space] * 4 + [vmem],
+        out_specs=[vmem] * 5,
         scratch_shapes=[
             pltpu.VMEM((2, ROWS, 2048), BF16),
             pltpu.VMEM((2, ROWS, 2048), BF16),
@@ -568,22 +538,13 @@
             dma((8,)),
         ],
         compiler_params=pltpu.CompilerParams(
-            collective_id=0, has_side_effects=True, vmem_limit_bytes=60 * 2**20
+            collective_id=0, has_side_effects=True, vmem_limit_bytes=56 * 2**20
         ),
         cost_estimate=pl.CostEstimate(
             flops=6 * 10**9, bytes_accessed=5 * 10**6, transcendentals=5 * 10**6
         ),
     )(queries, key_rows, value_rows, upstream, norm_gains, segments)
-    return tuple(
-        pl.pallas_call(
-            hand_over,
-            out_shape=shapes,
-            in_specs=[any_space] * 5,
-            out_specs=[any_space] * 5,
-            scratch_shapes=[pltpu.VMEM(one.shape, one.dtype) for one in shapes]
-            + [dma((20,)), dma((20,))],
-        )(*results)
-    )
+    return tuple(results)
 
 
 def solution(mesh):

time: 62.2 us -> 62.5 us (level)
  local copies, waits for them, and re-layouts: 0 us -> 3.81 us
  Pallas kernels: 61.3 us -> 57.9 us
    unnamed x0 -> x5, local copies, waits for them, and re-layouts: none -> 3.81 us
    pallas_call x2 -> x1, Pallas kernels: 61.3 us -> 57.9 us  [on_device(): pl.pallas_call(kernel, out_shape=[pltpu.VMEM(one.shape, one.dtype) for on...]
where the time goes in v1:
time: 62.5 us; the launch traced here: 62.3 us
  Pallas kernels  57.9 us (93%)
  local copies, waits for them, and re-layouts  3.81 us (6%)
  between operations  0.64 us (1%)
    pallas_call x1, Pallas kernels, on_device(): pl.pallas_call(kernel, out_shape=[pltpu.VMEM(one.shape, one.dtype) for on...  57.9 us
    unnamed x5, local copies, waits for them, and re-layouts  3.81 us

profile of v1, /device:TPU:1, one launch (start us, length us, event | category | flops | bytes accessed | tf_op | source)
XLA Modules:
  0.0 62.3 jit_solution(924424814463629357)
XLA Ops:
  0.6 57.9 %shard_map.101 = (bf16[1,128,4096]{2,1,0:T(8,128)(2,1)S(1)}, bf16[1,128,4096]{2,1,0:T(8,128)(2,1)S(1)}, bf16[1,128,512]{2,1,0:T(8,128)(2,1)S(1)}, bf16[1,128,512]{2,1,0:T(8,128)(2,1)S(1)}, f32[1,256]{1,0:T(1,128)S(1)}) custom-call(bf16[1,128,4096]{2,1,0:T(8,128)(2,1)} %queries.1, bf16[1,128,512]{2,1,0:T(8,128)(2,1)} %keys.1, bf16[1,128,512]{2,1,0:T(8,128)(2,1)} %values.1, ...), custom_call_target="tpu_custom_call" | custom-call | flops 6000000000 | bytes 5000000 | tf_op jit(solution)/shard_map/pallas_call | solution.py:501
  58.5 1.0 %copy.16 = bf16[1,128,4096]{2,1,0:T(8,128)(2,1)} copy(bf16[1,128,4096]{2,1,0:T(8,128)(2,1)S(1)} %get-tuple-element.5) | data formatting | bytes 2097152
  59.5 0.6 copy.20
  60.0 0.7 %copy.18 = bf16[1,128,512]{2,1,0:T(8,128)(2,1)} copy(bf16[1,128,512]{2,1,0:T(8,128)(2,1)S(1)} %get-tuple-element.7) | data formatting | bytes 262144
  60.7 0.7 %copy.19 = bf16[1,128,512]{2,1,0:T(8,128)(2,1)} copy(bf16[1,128,512]{2,1,0:T(8,128)(2,1)S(1)} %get-tuple-element.8) | data formatting | bytes 262144
  61.4 1.0 %copy.17 = bf16[1,128,4096]{2,1,0:T(8,128)(2,1)} copy(bf16[1,128,4096]{2,1,0:T(8,128)(2,1)S(1)} %get-tuple-element.6) | data formatting | bytes 2097152

commit v2 on v1

--- a/solution.py
+++ b/solution.py
@@ -168,6 +168,49 @@
         for j in range(2):
             own_copy(kind, j).start()
 
+    def first_copy(kind, cross):
+        rows = pl.ds(pl.multiple_of(2 * PAIR + core * ROWS, ROWS), ROWS)
+        return remote(
+            leaving(kind, 0, other if cross else core),
+            kv_raw.at[0, kind, rows, :],
+            gather_send.at[0, kind, 4 * cross],
+            gather_recv.at[0, kind, 4 * cross],
+            up_cross if cross else up_z,
+        )
+
+    def enter(j, kind):
+        own_copy(kind, j).wait()
+        core_copy(kind, j).wait_recv()
+        if j == 1:
+            gather_copy(j, kind, 0).start()
+
+    def pass_on(j, kind):
+        if j == 0:
+            first_copy(kind, 0).wait_recv()
+            first_copy(kind, 1).wait_recv()
+        else:
+            gather_copy(j, kind, 0).wait_recv()
+        gather_copy(j, kind, 1).start()
+        gather_copy(j, kind, 3).start()
+
+    pl.semaphore_wait(barrier, 17)
+    for kind in range(2):
+        for cross in range(2):
+            first_copy(kind, cross).start()
+    for j in range(2):
+        for kind in range(2):
+            core_copy(kind, j).start()
+    for j in range(2):
+        for kind in range(2, 4):
+            core_copy(kind, j).start()
+    for kind in range(2):
+        enter(0, kind)
+
+        @pl.when(col == 0)
+        def _():
+            gather_copy(0, kind, 2).start()
+
+
     pair_at = z * 2 + col
     pieces = []
     for piece in range(SPAN // 128):
@@ -191,48 +234,6 @@
     for j in range(2):
         own_copy(2, j).wait()
         prepare_queries(j, core)
-
-    def first_copy(kind, cross):
-        rows = pl.ds(pl.multiple_of(2 * PAIR + core * ROWS, ROWS), ROWS)
-        return remote(
-            leaving(kind, 0, other if cross else core),
-            kv_raw.at[0, kind, rows, :],
-            gather_send.at[0, kind, 4 * cross],
-            gather_recv.at[0, kind, 4 * cross],
-            up_cross if cross else up_z,
-        )
-
-    def enter(j, kind):
-        own_copy(kind, j).wait()
-        core_copy(kind, j).wait_recv()
-        if j == 1:
-            gather_copy(j, kind, 0).start()
-
-    def pass_on(j, kind):
-        if j == 0:
-            first_copy(kind, 0).wait_recv()
-            first_copy(kind, 1).wait_recv()
-        else:
-            gather_copy(j, kind, 0).wait_recv()
-        gather_copy(j, kind, 1).start()
-        gather_copy(j, kind, 3).start()
-
-    pl.semaphore_wait(barrier, 17)
-    for kind in range(2):
-        for cross in range(2):
-            first_copy(kind, cross).start()
-    for j in range(2):
-        for kind in range(2):
-            core_copy(kind, j).start()
-    for j in range(2):
-        for kind in range(2, 4):
-            core_copy(kind, j).start()
-    for kind in range(2):
-        enter(0, kind)
-
-        @pl.when(col == 0)
-        def _():
-            gather_copy(0, kind, 2).start()
 
     prepare_keys(0, 4)
     pass_on(0, 0)

time: 62.5 us -> 62.5 us (level)
  no operation moved by 1% of the time
where the time goes in v2:
time: 62.5 us; the launch traced here: 62.3 us
  Pallas kernels  57.9 us (93%)
  local copies, waits for them, and re-layouts  3.81 us (6%)
  between operations  0.64 us (1%)
    pallas_call x1, Pallas kernels, on_device(): pl.pallas_call(kernel, out_shape=[pltpu.VMEM(one.shape, one.dtype) for on...  57.9 us
    unnamed x5, local copies, waits for them, and re-layouts  3.81 us

profile of v2, /device:TPU:1, one launch (start us, length us, event | category | flops | bytes accessed | tf_op | source)
XLA Modules:
  0.0 62.3 jit_solution(9297963657547181780)
XLA Ops:
  0.6 57.9 %shard_map.101 = (bf16[1,128,4096]{2,1,0:T(8,128)(2,1)S(1)}, bf16[1,128,4096]{2,1,0:T(8,128)(2,1)S(1)}, bf16[1,128,512]{2,1,0:T(8,128)(2,1)S(1)}, bf16[1,128,512]{2,1,0:T(8,128)(2,1)S(1)}, f32[1,256]{1,0:T(1,128)S(1)}) custom-call(bf16[1,128,4096]{2,1,0:T(8,128)(2,1)} %queries.1, bf16[1,128,512]{2,1,0:T(8,128)(2,1)} %keys.1, bf16[1,128,512]{2,1,0:T(8,128)(2,1)} %values.1, ...), custom_call_target="tpu_custom_call" | custom-call | flops 6000000000 | bytes 5000000 | tf_op jit(solution)/shard_map/pallas_call | solution.py:502
  58.5 1.0 %copy.16 = bf16[1,128,4096]{2,1,0:T(8,128)(2,1)} copy(bf16[1,128,4096]{2,1,0:T(8,128)(2,1)S(1)} %get-tuple-element.5) | data formatting | bytes 2097152
  59.5 0.6 copy.20
  60.0 0.7 %copy.18 = bf16[1,128,512]{2,1,0:T(8,128)(2,1)} copy(bf16[1,128,512]{2,1,0:T(8,128)(2,1)S(1)} %get-tuple-element.7) | data formatting | bytes 262144
  60.7 0.7 %copy.19 = bf16[1,128,512]{2,1,0:T(8,128)(2,1)} copy(bf16[1,128,512]{2,1,0:T(8,128)(2,1)S(1)} %get-tuple-element.8) | data formatting | bytes 262144
  61.4 1.0 %copy.17 = bf16[1,128,4096]{2,1,0:T(8,128)(2,1)} copy(bf16[1,128,4096]{2,1,0:T(8,128)(2,1)S(1)} %get-tuple-element.6) | data formatting | bytes 2097152
